TPU v7x, 32 devices: a whole 2x2x4 slice. The times are simulated.
32 devices in a mesh: ctx: 8 (over z, x), grp: 4 (over y, core).
Axes of the slice: x: 2, y: 2, z: 4, core: 2. Of those that a mesh axis runs over, the one named last changes fastest.
Arguments:
- queries: bfloat16 [16384, 512], P('ctx', 'grp'), may hold values from -100 to 100
- kv_cache: bfloat16 [16384, 256], P(('ctx', 'grp')), may hold values from -6 to 6
- grad_out: bfloat16 [16384, 512], P('ctx', 'grp'), may hold values from -6 to 6
- doc_tiles: int32 [4], replicated, may hold values from 1 to 12, 32 in all
Outputs:
- grad_queries: bfloat16 [16384, 512], P('ctx', 'grp')
- grad_kv: bfloat16 [16384, 256], P(('ctx', 'grp'))
All inputs are finite; a program needn't handle non-finite values.
Results may differ from a plain program's by a relative error of at most 0.0059.
Values may be sent and summed in bfloat16 or wider, within the bound.
No kernel may reach another device: no remote copies, remote signals or barrier semaphores. Data moves between devices by JAX's collectives and lax.ppermute only.
A program may use at most 64 MiB of HBM per device.

v0:
```python
import math

import jax
import jax.numpy as jnp
from jax import lax
from jax.experimental import pallas as pl
from jax.experimental.pallas import tpu as pltpu
from jax.sharding import PartitionSpec as P

DH = 128
TILE = 512
MAXT = 12
NEG_FILL = -1e30
F32 = jnp.float32
BF16 = jnp.bfloat16


def to_bf16(x):
    return x.astype(BF16)


def fold_rows(x):
    return x.reshape(x.shape[0] // 8, 8, x.shape[1])


def first_tile_of(doc_ref, doc_count, tile):
    def step(d, carry):
        begin, found = carry
        found = jnp.where(begin <= tile, begin, found)
        return (begin + doc_ref[d], found)

    return lax.fori_loop(0, doc_count, step, (jnp.int32(0), jnp.int32(0)))[1]


def local_kernel(*refs, local_tiles, reach, scale):
    blocks = reach + 1
    doc_ref, q_ref, g_ref = refs[:3]
    piece_refs = refs[3 : 3 + 4 * blocks]
    dq_ref = refs[3 + 4 * blocks]
    out_refs = refs[4 + 4 * blocks : 4 + 6 * blocks]
    win, kt, scores, dprobs, tops, probs_low, ds_low, acc, dqt, sems = refs[4 + 6 * blocks :]

    slots = blocks * local_tiles
    c = lax.axis_index("ctx")
    g = lax.axis_index("grp")
    base = (c - reach) * local_tiles
    to_log2 = scale * math.log2(math.e)

    copies = []
    for b in range(blocks):
        for i in range(4):
            copies.append(
                pltpu.make_async_copy(
                    piece_refs[4 * b + i], win.at[b * local_tiles + (g ^ i)], sems.at[b, i]
                )
            )
    for copy in copies:
        copy.start()
    acc[...] = jnp.zeros_like(acc)
    for copy in copies:
        copy.wait()

    doc_count = doc_ref.shape[0]
    low = first_tile_of(doc_ref, doc_count, c * local_tiles) - base

    @pl.loop(low, slots)
    def _(j):
        kt[j] = win[j, :, :DH].T

    causal = lax.broadcasted_iota(jnp.int32, (TILE, TILE), 0) <= lax.broadcasted_iota(
        jnp.int32, (TILE, TILE), 1
    )

    @pl.loop(0, local_tiles)
    def _(t):
        rows = pl.ds(pl.multiple_of(t * TILE, TILE), TILE)
        q = q_ref[rows, :]
        go = g_ref[rows, :]
        qt = q.T
        gt = go.T
        diag = reach * local_tiles + t
        first = first_tile_of(doc_ref, doc_count, c * local_tiles + t) - base

        def make_scores(j, top, mask=None):
            s = jnp.dot(win[j, :, :DH], qt, preferred_element_type=F32) * to_log2
            if mask is not None:
                s = jnp.where(mask, s, NEG_FILL)
            scores[j - first] = s
            top = jnp.maximum(top, jnp.max(fold_rows(s), axis=0))
            tops[j - first] = top
            dprobs[j - first] = jnp.dot(win[j, :, DH:], gt, preferred_element_type=F32)
            return top

        def make_probs(j, older, newer, total, dsum):
            p = jnp.exp2(fold_rows(scores[j - first]) - newer[None])
            scores[j - first] = p.reshape(TILE, TILE)
            fade = jnp.exp2(older - newer)
            total = total * fade + jnp.sum(p, axis=0)
            dsum = dsum * fade + jnp.sum(p * fold_rows(dprobs[j - first]), axis=0)
            return total, dsum

        def forward_step(j, carry):
            last, older, newer, total, dsum = carry
            newest = make_scores(j, newer)
            total, dsum = make_probs(last, older, newer, total, dsum)
            return (j, newer, newest, total, dsum)

        zero = jnp.zeros((8, TILE), F32)
        floor = jnp.full((8, TILE), NEG_FILL, F32)
        carry = (diag, floor, make_scores(diag, floor, causal), zero, zero)
        last, older, newer, total, dsum = lax.fori_loop(first, diag, forward_step, carry)
        total, dsum = make_probs(last, older, newer, total, dsum)

        peak = jnp.max(newer, axis=0, keepdims=True)
        fade = jnp.exp2(newer - peak)
        inv = 1.0 / jnp.sum(total * fade, axis=0, keepdims=True)
        delta = jnp.sum(dsum * fade, axis=0, keepdims=True) * inv
        dqt[...] = jnp.zeros_like(dqt)

        def make_dscore(j, slot):
            factor = jnp.exp2(tops[j - first] - peak) * inv
            p = (fold_rows(scores[j - first]) * factor[None]).reshape(TILE, TILE)
            probs_low[slot] = to_bf16(p)
            ds_low[slot] = to_bf16(p * (dprobs[j - first] - delta))

        def make_grads(j, slot):
            ds = ds_low[slot]
            acc[j, :, DH:] += jnp.dot(probs_low[slot], go, preferred_element_type=F32)
            acc[j, :, :DH] += jnp.dot(ds, q, preferred_element_type=F32)
            dqt[...] += jnp.dot(kt[j], ds, preferred_element_type=F32)

        def backward_step(j, carry):
            last, slot = carry
            make_dscore(j, 1 - slot)
            make_grads(last, slot)
            return (j, 1 - slot)

        make_dscore(diag, 0)
        last, slot = lax.fori_loop(first, diag, backward_step, (diag, jnp.int32(0)))
        make_grads(last, slot)
        dq_ref[rows, :] = to_bf16((dqt[...] * scale).T)

    for b in range(blocks):
        for i in range(2):
            out_refs[2 * b][i] = to_bf16(acc[b * local_tiles + (g ^ (2 * i))])
            out_refs[2 * b + 1][i] = to_bf16(acc[b * local_tiles + (g ^ (2 * i + 1))])


def along_ctx(x, by):
    n = lax.axis_size("ctx")
    return lax.ppermute(x, "ctx", [(i, i + by) for i in range(n) if 0 <= i + by < n])


def swap_grp(x, bit):
    n = lax.axis_size("grp")
    return lax.ppermute(x, "grp", [(i, i ^ bit) for i in range(n)])


def shards(queries, kv_cache, grad_out, doc_tiles):
    local_tiles = queries.shape[0] // TILE
    reach = (MAXT - 2) // local_tiles + 1
    blocks = reach + 1
    slots = blocks * local_tiles
    scale = 1.0 / math.sqrt(DH)
    width = 2 * DH

    pieces = []
    for d in range(reach, -1, -1):
        x = along_ctx(kv_cache, d) if d else kv_cache
        y = swap_grp(x, 2)
        pieces += [x, swap_grp(x, 1), y, swap_grp(y, 1)]

    vmem = pl.BlockSpec(memory_space=pltpu.VMEM)
    hbm = pl.BlockSpec(memory_space=pl.ANY)
    half = jax.ShapeDtypeStruct((local_tiles // 2, TILE, width), BF16)
    grad_queries, *halves = pl.pallas_call(
        lambda *refs: local_kernel(*refs, local_tiles=local_tiles, reach=reach, scale=scale),
        out_shape=(jax.ShapeDtypeStruct(queries.shape, BF16),) + (half,) * (2 * blocks),
        in_specs=[pl.BlockSpec(memory_space=pltpu.SMEM), vmem, vmem] + [hbm] * (4 * blocks),
        out_specs=(vmem,) * (1 + 2 * blocks),
        scratch_shapes=[
            pltpu.VMEM((slots, TILE, width), BF16),
            pltpu.VMEM((slots, DH, TILE), BF16),
            pltpu.VMEM((MAXT, TILE, TILE), F32),
            pltpu.VMEM((MAXT, TILE, TILE), F32),
            pltpu.VMEM((MAXT, 8, TILE), F32),
            pltpu.VMEM((2, TILE, TILE), BF16),
            pltpu.VMEM((2, TILE, TILE), BF16),
            pltpu.VMEM((slots, TILE, width), F32),
            pltpu.VMEM((DH, TILE), F32),
            pltpu.SemaphoreType.DMA((blocks, 4)),
        ],
        compiler_params=pltpu.CompilerParams(vmem_limit_bytes=56 * 1024 * 1024),
    )(doc_tiles, queries, grad_out, *pieces)

    own = None
    for d in range(reach, -1, -1):
        keep, send = halves[2 * (reach - d)], halves[2 * (reach - d) + 1]
        got = swap_grp(send, 1).astype(F32)
        theirs = to_bf16(keep[1].astype(F32) + got[1])
        mine = keep[0].astype(F32) + got[0] + swap_grp(theirs, 2).astype(F32)
        if d:
            mine = along_ctx(to_bf16(mine), -d).astype(F32)
        own = mine if own is None else own + mine
    grad_kv = to_bf16(jnp.concatenate([own[:, :DH] * scale, own[:, DH:]], axis=1))
    return (grad_queries, grad_kv)


def solution(mesh):
    placed = (P("ctx", "grp"), P(("ctx", "grp"), None), P("ctx", "grp"), P())
    return jax.shard_map(
        shards,
        mesh=mesh,
        in_specs=placed,
        out_specs=(P("ctx", "grp"), P(("ctx", "grp"), None)),
        check_vma=False,
    )
```

profile of v0, /device:TPU:16, one launch (start us, length us, event | category | flops | bytes accessed | tf_op | source)
XLA Modules:
  0.0 134.3 jit_solution(1037654859665281863)
XLA Ops:
  0.6 3.4 %collective-permute-start.8 = (bf16[512,256]{1,0:T(8,128)(2,1)}, bf16[512,256]{1,0:T(8,128)(2,1)S(1)}, u32[]{:S(2)}, u32[]{:S(2)}) collective-permute-start(bf16[512,256]{1,0:T(8,128)(2,1)} %refs_15_.1), channel_id=1, source_target_pairs={{0,4},{4,8},{8,12},{12,16},{16,20},{20,24},{24,28},{1,5},{5,9},{9,... | collective-permute-start | bytes 786440 | tf_op jit(solution)/shard_map/ppermute | solution.py:151
  4.0 0.1 collective-permute-start.12
  4.1 3.5 %collective-permute-start.4 = (bf16[512,256]{1,0:T(8,128)(2,1)}, bf16[512,256]{1,0:T(8,128)(2,1)S(1)}, u32[]{:S(2)}, u32[]{:S(2)}) collective-permute-start(bf16[512,256]{1,0:T(8,128)(2,1)} %refs_15_.1), channel_id=1, source_target_pairs={{0,8},{4,12},{8,16},{12,20},{16,24},{20,28},{1,9},{5,13},{9,17},{1... | collective-permute-start | bytes 786440 | tf_op jit(solution)/shard_map/ppermute | solution.py:151
  7.6 1.9 %collective-permute-start = (bf16[512,256]{1,0:T(8,128)(2,1)}, bf16[512,256]{1,0:T(8,128)(2,1)S(1)}, u32[]{:S(2)}, u32[]{:S(2)}) collective-permute-start(bf16[512,256]{1,0:T(8,128)(2,1)} %refs_15_.1), channel_id=1, source_target_pairs={{0,12},{4,16},{8,20},{12,24},{16,28},{1,13},{5,17},{9,21},{13,25},... | collective-permute-start | bytes 786440 | tf_op jit(solution)/shard_map/ppermute | solution.py:151
  9.5 1.6 %collective-permute-start.13 = (bf16[512,256]{1,0:T(8,128)(2,1)}, bf16[512,256]{1,0:T(8,128)(2,1)S(1)}, u32[]{:S(2)}, u32[]{:S(2)}) collective-permute-start(bf16[512,256]{1,0:T(8,128)(2,1)} %refs_15_.1), channel_id=1, source_target_pairs={{0,2},{1,3},{2,0},{3,1},{4,6},{5,7},{6,4},{7,5},{8,10},{9,11},{10,... | collective-permute-start | bytes 786440 | tf_op jit(solution)/shard_map/ppermute | solution.py:156
  11.1 1.7 %collective-permute-done.8.refs_11_ = bf16[512,256]{1,0:T(8,128)(2,1)S(1)} collective-permute-done((bf16[512,256]{1,0:T(8,128)(2,1)}, bf16[512,256]{1,0:T(8,128)(2,1)S(1)}, u32[]{:S(2)}, u32[]{:S(2)}) %collective-permute-start.8) | collective-permute-done | bytes 262176 | tf_op jit(solution)/shard_map/ppermute | solution.py:151
  12.8 1.5 %collective-permute-start.10 = (bf16[512,256]{1,0:T(8,128)(2,1)S(1)}, bf16[512,256]{1,0:T(8,128)(2,1)S(1)}, u32[]{:S(2)}, u32[]{:S(2)}) collective-permute-start(bf16[512,256]{1,0:T(8,128)(2,1)S(1)} %collective-permute-done.8.refs_11_), channel_id=1, source_target_pairs={{0,2},{1,3},{2,0},{3,1},{4,6},{5,7},{6,4},{7,5},{8,10},{9,11},{10,... | collective-permute-start | bytes 786440 | tf_op jit(solution)/shard_map/ppermute | solution.py:156
  14.3 0.0 collective-permute-done.12.refs_16_
  14.4 0.0 collective-permute-start.9
  14.4 1.0 collective-permute-done.4.refs_7_
  15.3 1.5 %collective-permute-start.6 = (bf16[512,256]{1,0:T(8,128)(2,1)S(1)}, bf16[512,256]{1,0:T(8,128)(2,1)S(1)}, u32[]{:S(2)}, u32[]{:S(2)}) collective-permute-start(bf16[512,256]{1,0:T(8,128)(2,1)S(1)} %collective-permute-done.4.refs_7_), channel_id=1, source_target_pairs={{0,2},{1,3},{2,0},{3,1},{4,6},{5,7},{6,4},{7,5},{8,10},{9,11},{10,... | collective-permute-start | bytes 786440 | tf_op jit(solution)/shard_map/ppermute | solution.py:156
  16.8 6.1 %collective-permute-done.refs_3_ = bf16[512,256]{1,0:T(8,128)(2,1)S(1)} collective-permute-done((bf16[512,256]{1,0:T(8,128)(2,1)}, bf16[512,256]{1,0:T(8,128)(2,1)S(1)}, u32[]{:S(2)}, u32[]{:S(2)}) %collective-permute-start) | collective-permute-done | bytes 262176 | tf_op jit(solution)/shard_map/ppermute | solution.py:151
  22.9 0.0 collective-permute-start.5
  22.9 0.0 collective-permute-done.13.refs_17_
  22.9 1.6 %collective-permute-start.2 = (bf16[512,256]{1,0:T(8,128)(2,1)S(1)}, bf16[512,256]{1,0:T(8,128)(2,1)S(1)}, u32[]{:S(2)}, u32[]{:S(2)}) collective-permute-start(bf16[512,256]{1,0:T(8,128)(2,1)S(1)} %collective-permute-done.refs_3_), channel_id=1, source_target_pairs={{0,2},{1,3},{2,0},{3,1},{4,6},{5,7},{6,4},{7,5},{8,10},{9,11},{10,... | collective-permute-start | bytes 786440 | tf_op jit(solution)/shard_map/ppermute | solution.py:156
  24.5 0.1 collective-permute-done.10.refs_13_
  24.6 0.1 collective-permute-start.1
  24.7 0.0 collective-permute-done.9.refs_12_
  24.7 0.4 collective-permute-start.14
  25.1 5.1 %collective-permute-done.6.refs_9_ = bf16[512,256]{1,0:T(8,128)(2,1)S(1)} collective-permute-done((bf16[512,256]{1,0:T(8,128)(2,1)S(1)}, bf16[512,256]{1,0:T(8,128)(2,1)S(1)}, u32[]{:S(2)}, u32[]{:S(2)}) %collective-permute-start.6) | collective-permute-done | bytes 262176 | tf_op jit(solution)/shard_map/ppermute | solution.py:156
  30.2 0.0 collective-permute-start.11
  30.2 0.0 collective-permute-done.5.refs_8_
  30.2 0.5 collective-permute-start.7
  30.7 4.4 %collective-permute-done.2.refs_5_ = bf16[512,256]{1,0:T(8,128)(2,1)S(1)} collective-permute-done((bf16[512,256]{1,0:T(8,128)(2,1)S(1)}, bf16[512,256]{1,0:T(8,128)(2,1)S(1)}, u32[]{:S(2)}, u32[]{:S(2)}) %collective-permute-start.2) | collective-permute-done | bytes 262176 | tf_op jit(solution)/shard_map/ppermute | solution.py:156
  35.1 0.0 collective-permute-start.3
  35.1 0.0 collective-permute-done.1.refs_4_
  35.1 0.0 collective-permute-done.14.refs_18_
  35.1 0.0 collective-permute-done.11.refs_14_
  35.1 0.0 collective-permute-done.7.refs_10_
  35.2 1.5 %collective-permute-done.3.refs_6_ = bf16[512,256]{1,0:T(8,128)(2,1)S(1)} collective-permute-done((bf16[512,256]{1,0:T(8,128)(2,1)S(1)}, bf16[512,256]{1,0:T(8,128)(2,1)S(1)}, u32[]{:S(2)}, u32[]{:S(2)}) %collective-permute-start.3) | collective-permute-done | bytes 262176 | tf_op jit(solution)/shard_map/ppermute | solution.py:156
  36.7 0.7 copy-done.18
  37.5 21.2 %shard_map.59 = (bf16[2048,128]{1,0:T(8,128)(2,1)}, bf16[2,512,256]{2,1,0:T(8,128)(2,1)}, bf16[2,512,256]{2,1,0:T(8,128)(2,1)}, bf16[2,512,256]{2,1,0:T(8,128)(2...) custom-call(s32[4]{0:T(128)} %refs_0_.1, ...), custom_call_target="tpu_custom_call" | custom-call | tf_op jit(solution)/shard_map/pallas_call | solution.py:176
  58.7 0.2 collective-permute-start.15
  58.9 0.3 collective-permute-start.18
  59.3 0.2 collective-permute-start.21
  59.4 0.3 collective-permute-start.24
  59.8 1.1 collective-permute-done.15
  60.9 0.1 convert_element_type.100
  61.0 0.1 fusion.16
  61.0 1.7 %collective-permute-start.16 = (bf16[512,256]{1,0:T(8,128)(2,1)S(1)}, bf16[512,256]{1,0:T(8,128)(2,1)S(1)}, u32[]{:S(2)}, u32[]{:S(2)}) collective-permute-start(bf16[512,256]{1,0:T(8,128)(2,1)S(1)} %fusion.16), channel_id=1, source_target_pairs={{0,2},{1,3},{2,0},{3,1},{4,6},{5,7},{6,4},{7,5},{8,10},{9,11},{10,... | collective-permute-start | bytes 786440 | tf_op jit(solution)/shard_map/ppermute | solution.py:156
  62.7 0.1 convert_element_type.108
  62.8 0.1 fusion.17
  62.9 0.9 collective-permute-start.19
  63.8 0.0 collective-permute-done.21
  63.8 0.1 convert_element_type.116
  63.9 0.0 copy-done.1
  63.9 0.1 fusion.18
  64.0 1.2 collective-permute-start.22
  65.2 0.0 collective-permute-done.24
  65.2 0.1 convert_element_type.124
  65.3 0.1 fusion.19
  65.4 0.9 collective-permute-start.25
  66.3 3.9 %collective-permute-done.16 = bf16[512,256]{1,0:T(8,128)(2,1)S(1)} collective-permute-done((bf16[512,256]{1,0:T(8,128)(2,1)S(1)}, bf16[512,256]{1,0:T(8,128)(2,1)S(1)}, u32[]{:S(2)}, u32[]{:S(2)}) %collective-permute-start.16) | collective-permute-done | bytes 262176 | tf_op jit(solution)/shard_map/ppermute | solution.py:156
  70.2 0.1 fusion.15
  70.3 27.4 %collective-permute-start.17 = (bf16[512,256]{1,0:T(8,128)(2,1)S(1)}, bf16[512,256]{1,0:T(8,128)(2,1)S(1)}, u32[]{:S(2)}, u32[]{:S(2)}) collective-permute-start(bf16[512,256]{1,0:T(8,128)(2,1)S(1)} %fusion.15), channel_id=1, source_target_pairs={{12,0},{16,4},{20,8},{24,12},{28,16},{13,1},{17,5},{21,9},{25,13},... | collective-permute-start | bytes 786440 | tf_op jit(solution)/shard_map/ppermute | solution.py:151
  97.8 0.1 fusion.11
  97.9 25.4 %collective-permute-start.20 = (bf16[512,256]{1,0:T(8,128)(2,1)S(1)}, bf16[512,256]{1,0:T(8,128)(2,1)S(1)}, u32[]{:S(2)}, u32[]{:S(2)}) collective-permute-start(bf16[512,256]{1,0:T(8,128)(2,1)S(1)} %fusion.11), channel_id=1, source_target_pairs={{8,0},{12,4},{16,8},{20,12},{24,16},{28,20},{9,1},{13,5},{17,9},{2... | collective-permute-start | bytes 786440 | tf_op jit(solution)/shard_map/ppermute | solution.py:151
  123.3 0.1 fusion.7
  123.4 1.9 %collective-permute-start.23 = (bf16[512,256]{1,0:T(8,128)(2,1)S(1)}, bf16[512,256]{1,0:T(8,128)(2,1)S(1)}, u32[]{:S(2)}, u32[]{:S(2)}) collective-permute-start(bf16[512,256]{1,0:T(8,128)(2,1)S(1)} %fusion.7), channel_id=1, source_target_pairs={{4,0},{8,4},{12,8},{16,12},{20,16},{24,20},{28,24},{5,1},{9,5},{13... | collective-permute-start | bytes 786440 | tf_op jit(solution)/shard_map/ppermute | solution.py:151
  125.3 0.0 collective-permute-done.17
  125.3 4.7 %collective-permute-done.20 = bf16[512,256]{1,0:T(8,128)(2,1)S(1)} collective-permute-done((bf16[512,256]{1,0:T(8,128)(2,1)S(1)}, bf16[512,256]{1,0:T(8,128)(2,1)S(1)}, u32[]{:S(2)}, u32[]{:S(2)}) %collective-permute-start.20) | collective-permute-done | bytes 262176 | tf_op jit(solution)/shard_map/ppermute | solution.py:151
  130.0 3.3 %collective-permute-done.23 = bf16[512,256]{1,0:T(8,128)(2,1)S(1)} collective-permute-done((bf16[512,256]{1,0:T(8,128)(2,1)S(1)}, bf16[512,256]{1,0:T(8,128)(2,1)S(1)}, u32[]{:S(2)}, u32[]{:S(2)}) %collective-permute-start.23) | collective-permute-done | bytes 262176 | tf_op jit(solution)/shard_map/ppermute | solution.py:151
  133.3 0.2 fusion.3
  133.5 0.7 pad_maximum_fusion
  (42 shorter events, 0.1 us)
Async XLA Ops:
  0.6 12.2 %collective-permute-start.8 = (bf16[512,256]{1,0:T(8,128)(2,1)}, bf16[512,256]{1,0:T(8,128)(2,1)S(1)}, u32[]{:S(2)}, u32[]{:S(2)}) collective-permute-start(bf16[512,256]{1,0:T(8,128)(2,1)} %refs_15_.1), channel_id=1, source_target_pairs={{0,4},{4,8},{8,12},{12,16},{16,20},{20,24},{24,28},{1,5},{5,9},{9,... | collective-permute-start | bytes 786440 | tf_op jit(solution)/shard_map/ppermute | solution.py:151
  4.0 10.3 %collective-permute-start.12 = (bf16[512,256]{1,0:T(8,128)(2,1)}, bf16[512,256]{1,0:T(8,128)(2,1)S(1)}, u32[]{:S(2)}, u32[]{:S(2)}) collective-permute-start(bf16[512,256]{1,0:T(8,128)(2,1)} %refs_15_.1), channel_id=1, source_target_pairs={{0,1},{1,0},{2,3},{3,2},{4,5},{5,4},{6,7},{7,6},{8,9},{9,8},{10,11... | collective-permute-start | bytes 786440 | tf_op jit(solution)/shard_map/ppermute | solution.py:156
  4.1 11.2 %collective-permute-start.4 = (bf16[512,256]{1,0:T(8,128)(2,1)}, bf16[512,256]{1,0:T(8,128)(2,1)S(1)}, u32[]{:S(2)}, u32[]{:S(2)}) collective-permute-start(bf16[512,256]{1,0:T(8,128)(2,1)} %refs_15_.1), channel_id=1, source_target_pairs={{0,8},{4,12},{8,16},{12,20},{16,24},{20,28},{1,9},{5,13},{9,17},{1... | collective-permute-start | bytes 786440 | tf_op jit(solution)/shard_map/ppermute | solution.py:151
  7.6 15.3 %collective-permute-start = (bf16[512,256]{1,0:T(8,128)(2,1)}, bf16[512,256]{1,0:T(8,128)(2,1)S(1)}, u32[]{:S(2)}, u32[]{:S(2)}) collective-permute-start(bf16[512,256]{1,0:T(8,128)(2,1)} %refs_15_.1), channel_id=1, source_target_pairs={{0,12},{4,16},{8,20},{12,24},{16,28},{1,13},{5,17},{9,21},{13,25},... | collective-permute-start | bytes 786440 | tf_op jit(solution)/shard_map/ppermute | solution.py:151
  9.5 13.4 %collective-permute-start.13 = (bf16[512,256]{1,0:T(8,128)(2,1)}, bf16[512,256]{1,0:T(8,128)(2,1)S(1)}, u32[]{:S(2)}, u32[]{:S(2)}) collective-permute-start(bf16[512,256]{1,0:T(8,128)(2,1)} %refs_15_.1), channel_id=1, source_target_pairs={{0,2},{1,3},{2,0},{3,1},{4,6},{5,7},{6,4},{7,5},{8,10},{9,11},{10,... | collective-permute-start | bytes 786440 | tf_op jit(solution)/shard_map/ppermute | solution.py:156
  12.8 23.8 %copy-start.4 = (bf16[512,256]{1,0:T(8,128)(2,1)}, bf16[512,256]{1,0:T(8,128)(2,1)S(1)}, u32[]{:S(2)}) copy-start(bf16[512,256]{1,0:T(8,128)(2,1)S(1)} %collective-permute-done.8.refs_11_) | copy-start | bytes 786436
  12.8 11.7 %collective-permute-start.10 = (bf16[512,256]{1,0:T(8,128)(2,1)S(1)}, bf16[512,256]{1,0:T(8,128)(2,1)S(1)}, u32[]{:S(2)}, u32[]{:S(2)}) collective-permute-start(bf16[512,256]{1,0:T(8,128)(2,1)S(1)} %collective-permute-done.8.refs_11_), channel_id=1, source_target_pairs={{0,2},{1,3},{2,0},{3,1},{4,6},{5,7},{6,4},{7,5},{8,10},{9,11},{10,... | collective-permute-start | bytes 786440 | tf_op jit(solution)/shard_map/ppermute | solution.py:156
  14.4 22.3 %copy-start.5 = (bf16[512,256]{1,0:T(8,128)(2,1)}, bf16[512,256]{1,0:T(8,128)(2,1)S(1)}, u32[]{:S(2)}) copy-start(bf16[512,256]{1,0:T(8,128)(2,1)S(1)} %collective-permute-done.12.refs_16_) | copy-start | bytes 786436
  14.4 10.3 %collective-permute-start.9 = (bf16[512,256]{1,0:T(8,128)(2,1)S(1)}, bf16[512,256]{1,0:T(8,128)(2,1)S(1)}, u32[]{:S(2)}, u32[]{:S(2)}) collective-permute-start(bf16[512,256]{1,0:T(8,128)(2,1)S(1)} %collective-permute-done.8.refs_11_), channel_id=1, source_target_pairs={{0,1},{1,0},{2,3},{3,2},{4,5},{5,4},{6,7},{7,6},{8,9},{9,8},{10,11... | collective-permute-start | bytes 786440 | tf_op jit(solution)/shard_map/ppermute | solution.py:156
  15.3 21.3 %copy-start.6 = (bf16[512,256]{1,0:T(8,128)(2,1)}, bf16[512,256]{1,0:T(8,128)(2,1)S(1)}, u32[]{:S(2)}) copy-start(bf16[512,256]{1,0:T(8,128)(2,1)S(1)} %collective-permute-done.4.refs_7_) | copy-start | bytes 786436
  15.3 14.9 %collective-permute-start.6 = (bf16[512,256]{1,0:T(8,128)(2,1)S(1)}, bf16[512,256]{1,0:T(8,128)(2,1)S(1)}, u32[]{:S(2)}, u32[]{:S(2)}) collective-permute-start(bf16[512,256]{1,0:T(8,128)(2,1)S(1)} %collective-permute-done.4.refs_7_), channel_id=1, source_target_pairs={{0,2},{1,3},{2,0},{3,1},{4,6},{5,7},{6,4},{7,5},{8,10},{9,11},{10,... | collective-permute-start | bytes 786440 | tf_op jit(solution)/shard_map/ppermute | solution.py:156
  22.9 13.7 %copy-start.7 = (bf16[512,256]{1,0:T(8,128)(2,1)}, bf16[512,256]{1,0:T(8,128)(2,1)S(1)}, u32[]{:S(2)}) copy-start(bf16[512,256]{1,0:T(8,128)(2,1)S(1)} %collective-permute-done.refs_3_) | copy-start | bytes 786436
  22.9 7.3 %collective-permute-start.5 = (bf16[512,256]{1,0:T(8,128)(2,1)S(1)}, bf16[512,256]{1,0:T(8,128)(2,1)S(1)}, u32[]{:S(2)}, u32[]{:S(2)}) collective-permute-start(bf16[512,256]{1,0:T(8,128)(2,1)S(1)} %collective-permute-done.4.refs_7_), channel_id=1, source_target_pairs={{0,1},{1,0},{2,3},{3,2},{4,5},{5,4},{6,7},{7,6},{8,9},{9,8},{10,11... | collective-permute-start | bytes 786440 | tf_op jit(solution)/shard_map/ppermute | solution.py:156
  22.9 13.7 %copy-start.8 = (bf16[512,256]{1,0:T(8,128)(2,1)}, bf16[512,256]{1,0:T(8,128)(2,1)S(1)}, u32[]{:S(2)}) copy-start(bf16[512,256]{1,0:T(8,128)(2,1)S(1)} %collective-permute-done.13.refs_17_) | copy-start | bytes 786436
  22.9 12.2 %collective-permute-start.2 = (bf16[512,256]{1,0:T(8,128)(2,1)S(1)}, bf16[512,256]{1,0:T(8,128)(2,1)S(1)}, u32[]{:S(2)}, u32[]{:S(2)}) collective-permute-start(bf16[512,256]{1,0:T(8,128)(2,1)S(1)} %collective-permute-done.refs_3_), channel_id=1, source_target_pairs={{0,2},{1,3},{2,0},{3,1},{4,6},{5,7},{6,4},{7,5},{8,10},{9,11},{10,... | collective-permute-start | bytes 786440 | tf_op jit(solution)/shard_map/ppermute | solution.py:156
  24.6 12.1 %copy-start.9 = (bf16[512,256]{1,0:T(8,128)(2,1)}, bf16[512,256]{1,0:T(8,128)(2,1)S(1)}, u32[]{:S(2)}) copy-start(bf16[512,256]{1,0:T(8,128)(2,1)S(1)} %collective-permute-done.10.refs_13_) | copy-start | bytes 786436
  24.6 10.5 %collective-permute-start.1 = (bf16[512,256]{1,0:T(8,128)(2,1)S(1)}, bf16[512,256]{1,0:T(8,128)(2,1)S(1)}, u32[]{:S(2)}, u32[]{:S(2)}) collective-permute-start(bf16[512,256]{1,0:T(8,128)(2,1)S(1)} %collective-permute-done.refs_3_), channel_id=1, source_target_pairs={{0,1},{1,0},{2,3},{3,2},{4,5},{5,4},{6,7},{7,6},{8,9},{9,8},{10,11... | collective-permute-start | bytes 786440 | tf_op jit(solution)/shard_map/ppermute | solution.py:156
  24.7 12.0 %copy-start.10 = (bf16[512,256]{1,0:T(8,128)(2,1)}, bf16[512,256]{1,0:T(8,128)(2,1)S(1)}, u32[]{:S(2)}) copy-start(bf16[512,256]{1,0:T(8,128)(2,1)S(1)} %collective-permute-done.9.refs_12_) | copy-start | bytes 786436
  24.7 10.4 %collective-permute-start.14 = (bf16[512,256]{1,0:T(8,128)(2,1)S(1)}, bf16[512,256]{1,0:T(8,128)(2,1)S(1)}, u32[]{:S(2)}, u32[]{:S(2)}) collective-permute-start(bf16[512,256]{1,0:T(8,128)(2,1)S(1)} %collective-permute-done.13.refs_17_), channel_id=1, source_target_pairs={{0,1},{1,0},{2,3},{3,2},{4,5},{5,4},{6,7},{7,6},{8,9},{9,8},{10,11... | collective-permute-start | bytes 786440 | tf_op jit(solution)/shard_map/ppermute | solution.py:156
  30.2 6.5 %copy-start.11 = (bf16[512,256]{1,0:T(8,128)(2,1)}, bf16[512,256]{1,0:T(8,128)(2,1)S(1)}, u32[]{:S(2)}) copy-start(bf16[512,256]{1,0:T(8,128)(2,1)S(1)} %collective-permute-done.6.refs_9_) | copy-start | bytes 786436
  30.2 4.9 %collective-permute-start.11 = (bf16[512,256]{1,0:T(8,128)(2,1)S(1)}, bf16[512,256]{1,0:T(8,128)(2,1)S(1)}, u32[]{:S(2)}, u32[]{:S(2)}) collective-permute-start(bf16[512,256]{1,0:T(8,128)(2,1)S(1)} %collective-permute-done.10.refs_13_), channel_id=1, source_target_pairs={{0,1},{1,0},{2,3},{3,2},{4,5},{5,4},{6,7},{7,6},{8,9},{9,8},{10,11... | collective-permute-start | bytes 786440 | tf_op jit(solution)/shard_map/ppermute | solution.py:156
  30.2 6.5 %copy-start.12 = (bf16[512,256]{1,0:T(8,128)(2,1)}, bf16[512,256]{1,0:T(8,128)(2,1)S(1)}, u32[]{:S(2)}) copy-start(bf16[512,256]{1,0:T(8,128)(2,1)S(1)} %collective-permute-done.5.refs_8_) | copy-start | bytes 786436
  30.2 4.9 %collective-permute-start.7 = (bf16[512,256]{1,0:T(8,128)(2,1)S(1)}, bf16[512,256]{1,0:T(8,128)(2,1)S(1)}, u32[]{:S(2)}, u32[]{:S(2)}) collective-permute-start(bf16[512,256]{1,0:T(8,128)(2,1)S(1)} %collective-permute-done.6.refs_9_), channel_id=1, source_target_pairs={{0,1},{1,0},{2,3},{3,2},{4,5},{5,4},{6,7},{7,6},{8,9},{9,8},{10,11... | collective-permute-start | bytes 786440 | tf_op jit(solution)/shard_map/ppermute | solution.py:156
  35.1 1.6 %copy-start.13 = (bf16[512,256]{1,0:T(8,128)(2,1)}, bf16[512,256]{1,0:T(8,128)(2,1)S(1)}, u32[]{:S(2)}) copy-start(bf16[512,256]{1,0:T(8,128)(2,1)S(1)} %collective-permute-done.2.refs_5_) | copy-start | bytes 786436
  35.1 1.5 %collective-permute-start.3 = (bf16[512,256]{1,0:T(8,128)(2,1)S(1)}, bf16[512,256]{1,0:T(8,128)(2,1)S(1)}, u32[]{:S(2)}, u32[]{:S(2)}) collective-permute-start(bf16[512,256]{1,0:T(8,128)(2,1)S(1)} %collective-permute-done.2.refs_5_), channel_id=1, source_target_pairs={{0,1},{1,0},{2,3},{3,2},{4,5},{5,4},{6,7},{7,6},{8,9},{9,8},{10,11... | collective-permute-start | bytes 786440 | tf_op jit(solution)/shard_map/ppermute | solution.py:156
  35.1 1.6 %copy-start.14 = (bf16[512,256]{1,0:T(8,128)(2,1)}, bf16[512,256]{1,0:T(8,128)(2,1)S(1)}, u32[]{:S(2)}) copy-start(bf16[512,256]{1,0:T(8,128)(2,1)S(1)} %collective-permute-done.1.refs_4_) | copy-start | bytes 786436
  35.1 1.6 %copy-start.15 = (bf16[512,256]{1,0:T(8,128)(2,1)}, bf16[512,256]{1,0:T(8,128)(2,1)S(1)}, u32[]{:S(2)}) copy-start(bf16[512,256]{1,0:T(8,128)(2,1)S(1)} %collective-permute-done.14.refs_18_) | copy-start | bytes 786436
  35.1 1.6 %copy-start.16 = (bf16[512,256]{1,0:T(8,128)(2,1)}, bf16[512,256]{1,0:T(8,128)(2,1)S(1)}, u32[]{:S(2)}) copy-start(bf16[512,256]{1,0:T(8,128)(2,1)S(1)} %collective-permute-done.11.refs_14_) | copy-start | bytes 786436
  35.2 1.6 %copy-start.17 = (bf16[512,256]{1,0:T(8,128)(2,1)}, bf16[512,256]{1,0:T(8,128)(2,1)S(1)}, u32[]{:S(2)}) copy-start(bf16[512,256]{1,0:T(8,128)(2,1)S(1)} %collective-permute-done.7.refs_10_) | copy-start | bytes 786436
  36.7 0.7 copy-start.18
  58.7 2.2 %collective-permute-start.15 = (bf16[2,512,256]{2,1,0:T(8,128)(2,1)}, bf16[2,512,256]{2,1,0:T(8,128)(2,1)S(1)}, u32[]{:S(2)}, u32[]{:S(2)}) collective-permute-start(bf16[2,512,256]{2,1,0:T(8,128)(2,1)} %get-tuple-element.13), channel_id=1, source_target_pairs={{0,1},{1,0},{2,3},{3,2},{4,5},{5,4},{6,7},{7,6},{8,9},{9,8},{10,11... | collective-permute-start | bytes 1572872 | tf_op jit(solution)/shard_map/ppermute | solution.py:156
  58.9 3.8 %collective-permute-start.18 = (bf16[2,512,256]{2,1,0:T(8,128)(2,1)}, bf16[2,512,256]{2,1,0:T(8,128)(2,1)S(1)}, u32[]{:S(2)}, u32[]{:S(2)}) collective-permute-start(bf16[2,512,256]{2,1,0:T(8,128)(2,1)} %get-tuple-element.15), channel_id=1, source_target_pairs={{0,1},{1,0},{2,3},{3,2},{4,5},{5,4},{6,7},{7,6},{8,9},{9,8},{10,11... | collective-permute-start | bytes 1572872 | tf_op jit(solution)/shard_map/ppermute | solution.py:156
  59.3 4.6 %collective-permute-start.21 = (bf16[2,512,256]{2,1,0:T(8,128)(2,1)}, bf16[2,512,256]{2,1,0:T(8,128)(2,1)S(1)}, u32[]{:S(2)}, u32[]{:S(2)}) collective-permute-start(bf16[2,512,256]{2,1,0:T(8,128)(2,1)} %get-tuple-element.17), channel_id=1, source_target_pairs={{0,1},{1,0},{2,3},{3,2},{4,5},{5,4},{6,7},{7,6},{8,9},{9,8},{10,11... | collective-permute-start | bytes 1572872 | tf_op jit(solution)/shard_map/ppermute | solution.py:156
  59.4 1.5 %copy-start.3 = (bf16[2,512,256]{2,1,0:T(8,128)(2,1)S(1)}, bf16[2,512,256]{2,1,0:T(8,128)(2,1)}, u32[]{:S(2)}) copy-start(bf16[2,512,256]{2,1,0:T(8,128)(2,1)} %get-tuple-element.12) | copy-start | bytes 1572868
  59.4 5.8 %collective-permute-start.24 = (bf16[2,512,256]{2,1,0:T(8,128)(2,1)}, bf16[2,512,256]{2,1,0:T(8,128)(2,1)S(1)}, u32[]{:S(2)}, u32[]{:S(2)}) collective-permute-start(bf16[2,512,256]{2,1,0:T(8,128)(2,1)} %get-tuple-element.19), channel_id=1, source_target_pairs={{0,1},{1,0},{2,3},{3,2},{4,5},{5,4},{6,7},{7,6},{8,9},{9,8},{10,11... | collective-permute-start | bytes 1572872 | tf_op jit(solution)/shard_map/ppermute | solution.py:156
  61.0 1.8 %copy-start.2 = (bf16[2,512,256]{2,1,0:T(8,128)(2,1)S(1)}, bf16[2,512,256]{2,1,0:T(8,128)(2,1)}, u32[]{:S(2)}) copy-start(bf16[2,512,256]{2,1,0:T(8,128)(2,1)} %get-tuple-element.14) | copy-start | bytes 1572868
  61.0 9.2 %collective-permute-start.16 = (bf16[512,256]{1,0:T(8,128)(2,1)S(1)}, bf16[512,256]{1,0:T(8,128)(2,1)S(1)}, u32[]{:S(2)}, u32[]{:S(2)}) collective-permute-start(bf16[512,256]{1,0:T(8,128)(2,1)S(1)} %fusion.16), channel_id=1, source_target_pairs={{0,2},{1,3},{2,0},{3,1},{4,6},{5,7},{6,4},{7,5},{8,10},{9,11},{10,... | collective-permute-start | bytes 786440 | tf_op jit(solution)/shard_map/ppermute | solution.py:156
  62.9 1.0 copy-start.1
  62.9 34.9 %collective-permute-start.19 = (bf16[512,256]{1,0:T(8,128)(2,1)S(1)}, bf16[512,256]{1,0:T(8,128)(2,1)S(1)}, u32[]{:S(2)}, u32[]{:S(2)}) collective-permute-start(bf16[512,256]{1,0:T(8,128)(2,1)S(1)} %fusion.17), channel_id=1, source_target_pairs={{0,2},{1,3},{2,0},{3,1},{4,6},{5,7},{6,4},{7,5},{8,10},{9,11},{10,... | collective-permute-start | bytes 786440 | tf_op jit(solution)/shard_map/ppermute | solution.py:156
  64.0 1.3 copy-start
  64.0 59.3 %collective-permute-start.22 = (bf16[512,256]{1,0:T(8,128)(2,1)S(1)}, bf16[512,256]{1,0:T(8,128)(2,1)S(1)}, u32[]{:S(2)}, u32[]{:S(2)}) collective-permute-start(bf16[512,256]{1,0:T(8,128)(2,1)S(1)} %fusion.18), channel_id=1, source_target_pairs={{0,2},{1,3},{2,0},{3,1},{4,6},{5,7},{6,4},{7,5},{8,10},{9,11},{10,... | collective-permute-start | bytes 786440 | tf_op jit(solution)/shard_map/ppermute | solution.py:156
  65.4 59.9 %collective-permute-start.25 = (bf16[512,256]{1,0:T(8,128)(2,1)S(1)}, bf16[512,256]{1,0:T(8,128)(2,1)S(1)}, u32[]{:S(2)}, u32[]{:S(2)}) collective-permute-start(bf16[512,256]{1,0:T(8,128)(2,1)S(1)} %fusion.19), channel_id=1, source_target_pairs={{0,2},{1,3},{2,0},{3,1},{4,6},{5,7},{6,4},{7,5},{8,10},{9,11},{10,... | collective-permute-start | bytes 786440 | tf_op jit(solution)/shard_map/ppermute | solution.py:156
  70.3 55.0 %collective-permute-start.17 = (bf16[512,256]{1,0:T(8,128)(2,1)S(1)}, bf16[512,256]{1,0:T(8,128)(2,1)S(1)}, u32[]{:S(2)}, u32[]{:S(2)}) collective-permute-start(bf16[512,256]{1,0:T(8,128)(2,1)S(1)} %fusion.15), channel_id=1, source_target_pairs={{12,0},{16,4},{20,8},{24,12},{28,16},{13,1},{17,5},{21,9},{25,13},... | collective-permute-start | bytes 786440 | tf_op jit(solution)/shard_map/ppermute | solution.py:151
  97.9 32.1 %collective-permute-start.20 = (bf16[512,256]{1,0:T(8,128)(2,1)S(1)}, bf16[512,256]{1,0:T(8,128)(2,1)S(1)}, u32[]{:S(2)}, u32[]{:S(2)}) collective-permute-start(bf16[512,256]{1,0:T(8,128)(2,1)S(1)} %fusion.11), channel_id=1, source_target_pairs={{8,0},{12,4},{16,8},{20,12},{24,16},{28,20},{9,1},{13,5},{17,9},{2... | collective-permute-start | bytes 786440 | tf_op jit(solution)/shard_map/ppermute | solution.py:151
  123.4 9.9 %collective-permute-start.23 = (bf16[512,256]{1,0:T(8,128)(2,1)S(1)}, bf16[512,256]{1,0:T(8,128)(2,1)S(1)}, u32[]{:S(2)}, u32[]{:S(2)}) collective-permute-start(bf16[512,256]{1,0:T(8,128)(2,1)S(1)} %fusion.7), channel_id=1, source_target_pairs={{4,0},{8,4},{12,8},{16,12},{20,16},{24,20},{28,24},{5,1},{9,5},{13... | collective-permute-start | bytes 786440 | tf_op jit(solution)/shard_map/ppermute | solution.py:151
where the time goes:
time: 137 us; the launch traced here: 134 us
  starting transfers between devices  76.7 us (56%)
  waiting for transfers between devices  32.8 us (24%)
  Pallas kernels  21.2 us (15%)
  other arithmetic  1.73 us (1%)
    ppermute x6, starting transfers between devices, along_ctx(): lax.ppermute(x, 'ctx', [(i, i + by) for i in range(n) if 0 <= i + by < n])  63.5 us
    pallas_call x1, Pallas kernels, shards(): pl.pallas_call(lambda *refs: local_kernel(*refs, local_tiles=local_tiles,...  21.2 us
    ppermute x6, waiting for transfers between devices, along_ctx(): lax.ppermute(x, 'ctx', [(i, i + by) for i in range(n) if 0 <= i + by < n])  16.7 us
    ppermute x20, waiting for transfers between devices, swap_grp(): return lax.ppermute(x, 'grp', [(i, i ^ bit) for i in range(n)])  16.1 us
    ppermute x20, starting transfers between devices, swap_grp(): return lax.ppermute(x, 'grp', [(i, i ^ bit) for i in range(n)])  13.1 us
  transfers between devices with their start and end apart: 26, of which 11 were waited for; matrix products, arithmetic and copies ran while one was open for 1% of the time, Pallas kernels for 0%

commit v1 on v0

v1 whole, which is shorter than its diff:
```python
import math

import jax
import jax.numpy as jnp
from jax import lax
from jax.experimental import pallas as pl
from jax.experimental.pallas import tpu as pltpu
from jax.sharding import PartitionSpec as P

DH = 128
TILE = 512
MAXT = 12
NEG_FILL = -1e30
HUGE = 2.0**100
F32 = jnp.float32
BF16 = jnp.bfloat16


def to_bf16(x):
    return x.astype(BF16)


def fold_rows(x):
    return x.reshape(x.shape[0] // 8, 8, x.shape[1])


def first_tile_of(doc_ref, doc_count, tile):
    def step(d, carry):
        begin, found = carry
        found = jnp.where(begin <= tile, begin, found)
        return (begin + doc_ref[d], found)

    return lax.fori_loop(0, doc_count, step, (jnp.int32(0), jnp.int32(0)))[1]


def local_kernel(*refs, local_tiles, reach, scale):
    blocks = reach + 1
    doc_ref, q_hbm, g_hbm = refs[:3]
    piece_refs = refs[3 : 3 + 4 * blocks]
    dq_hbm = refs[3 + 4 * blocks]
    out_refs = refs[4 + 4 * blocks : 4 + 6 * blocks]
    q_ref, g_ref, dq_ref, win, kt, scores, dprobs, acc, dqt, sems, io_sems = refs[4 + 6 * blocks :]

    slots = blocks * local_tiles
    c = lax.axis_index("ctx")
    g = lax.axis_index("grp")
    base = (c - reach) * local_tiles
    to_log2 = scale * math.log2(math.e)

    def tile_rows(b, owner):
        return pl.ds(pl.multiple_of((b * local_tiles + owner) * TILE, TILE), TILE)

    copies = [
        pltpu.make_async_copy(q_hbm, q_ref, io_sems.at[0]),
        pltpu.make_async_copy(g_hbm, g_ref, io_sems.at[1]),
    ]
    for b in range(blocks):
        for i in range(4):
            copies.append(
                pltpu.make_async_copy(
                    piece_refs[4 * b + i], win.at[tile_rows(b, g ^ i)], sems.at[b, i]
                )
            )
    for copy in copies:
        copy.start()
    acc[...] = jnp.zeros_like(acc)
    for copy in copies:
        copy.wait()

    doc_count = doc_ref.shape[0]
    low = first_tile_of(doc_ref, doc_count, c * local_tiles) - base

    @pl.loop(low, slots)
    def _(j):
        kt[j] = win[pl.ds(pl.multiple_of(j * TILE, TILE), TILE), :DH].T

    half = TILE // 2
    causal = lax.broadcasted_iota(jnp.int32, (half, half), 0) <= lax.broadcasted_iota(
        jnp.int32, (half, half), 1
    )

    def widen_lanes(x):
        return jnp.concatenate([jnp.zeros_like(x), x], axis=1)

    @pl.loop(0, local_tiles)
    def _(t):
        rows = pl.ds(pl.multiple_of(t * TILE, TILE), TILE)
        q = q_ref[rows, :]
        go = g_ref[rows, :]
        qt = q.T
        gt = go.T
        diag = reach * local_tiles + t
        first = first_tile_of(doc_ref, doc_count, c * local_tiles + t) - base

        def key_rows(j, count):
            return pl.ds(pl.multiple_of(j * TILE, TILE), count * TILE)

        def in_steps(step, carry):
            doubles = (diag - first) // 2
            carry = lax.fori_loop(
                0, doubles, lambda i, x: step(first + 2 * i, 2, x), carry
            )
            return lax.fori_loop(first + 2 * doubles, diag, lambda j, x: step(j, 1, x), carry)

        def raw_scores(at, queries_t):
            return jnp.dot(win[at, :DH], queries_t, preferred_element_type=F32) * to_log2

        upper = pl.ds(pl.multiple_of(diag * TILE, half), half)
        lower = pl.ds(pl.multiple_of(diag * TILE + half, half), half)
        slot = diag - first
        upper_to = pl.ds(pl.multiple_of(slot * TILE, half), half)
        lower_to = pl.ds(pl.multiple_of(slot * TILE + half, half), half)

        def diag_scores():
            s0 = raw_scores(upper, qt)
            s0 = jnp.concatenate(
                [jnp.where(causal, s0[:, :half], NEG_FILL), s0[:, half:]], axis=1
            )
            s1 = jnp.where(causal, raw_scores(lower, qt[:, half:]), NEG_FILL)
            return s0, s1

        def sums_of(p, dp):
            return jnp.sum(fold_rows(p), axis=0), jnp.sum(fold_rows(p * dp), axis=0)

        def forward(ref, s0, s1):
            def step(j, count, carry):
                total, dsum = carry
                at = key_rows(j, count)
                to = key_rows(j - first, count)
                p = jnp.exp2(raw_scores(at, qt) - ref)
                scores[to, :] = p
                dp = jnp.dot(win[at, DH:], gt, preferred_element_type=F32)
                dprobs[to, :] = dp
                more, dmore = sums_of(p, dp)
                return (total + more, dsum + dmore)

            p0 = jnp.exp2(s0 - ref)
            p1 = jnp.exp2(s1 - ref[:, half:])
            dp0 = jnp.dot(win[upper, DH:], gt, preferred_element_type=F32)
            dp1 = jnp.dot(win[lower, DH:], gt[:, half:], preferred_element_type=F32)
            scores[upper_to, :] = p0
            scores[lower_to, half:] = p1
            dprobs[upper_to, :] = dp0
            dprobs[lower_to, half:] = dp1
            total0, dsum0 = sums_of(p0, dp0)
            total1, dsum1 = sums_of(p1, dp1)
            total, dsum = in_steps(
                step, (total0 + widen_lanes(total1), dsum0 + widen_lanes(dsum1))
            )
            return jnp.sum(total, axis=0, keepdims=True), jnp.sum(dsum, axis=0, keepdims=True)

        def diag_top(s0, s1):
            top0 = jnp.max(s0, axis=0, keepdims=True)
            top1 = jnp.max(s1, axis=0, keepdims=True)
            return jnp.concatenate(
                [top0[:, :half], jnp.maximum(top0[:, half:], top1)], axis=1
            )

        def exact():
            def step(j, count, top):
                s = raw_scores(key_rows(j, count), qt)
                return jnp.maximum(top, jnp.max(s, axis=0, keepdims=True))

            s0, s1 = diag_scores()
            return forward(in_steps(step, diag_top(s0, s1)), s0, s1)

        s0, s1 = diag_scores()
        total, dsum = forward(diag_top(s0, s1), s0, s1)
        fits = jnp.max(jnp.where(total < HUGE, 0.0, 1.0)) == 0.0
        total, dsum = lax.cond(fits, lambda: (total, dsum), exact)

        inv = 1.0 / total
        delta = dsum * inv
        dqt[...] = jnp.zeros_like(dqt)

        def grads(p, dp, inv, delta):
            p = p * inv
            return to_bf16(p), to_bf16(p * (dp - delta))

        def add_grads(at, low, ds, q, go):
            acc[at, DH:] += jnp.dot(low, go, preferred_element_type=F32)
            acc[at, :DH] += jnp.dot(ds, q, preferred_element_type=F32)

        def backward(j, count, carry):
            at = key_rows(j, count)
            to = key_rows(j - first, count)
            low, ds = grads(scores[to, :], dprobs[to, :], inv, delta)
            add_grads(at, low, ds, q, go)
            part = dqt[...]
            for i in range(count):
                part += jnp.dot(
                    kt[j + i], ds[i * TILE : (i + 1) * TILE], preferred_element_type=F32
                )
            dqt[...] = part
            return carry

        low0, ds0 = grads(scores[upper_to, :], dprobs[upper_to, :], inv, delta)
        low1, ds1 = grads(
            scores[lower_to, half:], dprobs[lower_to, half:], inv[:, half:], delta[:, half:]
        )
        add_grads(upper, low0, ds0, q, go)
        add_grads(lower, low1, ds1, q[half:], go[half:])
        dqt[...] = jnp.dot(kt[diag, :, :half], ds0, preferred_element_type=F32)
        dqt[:, half:] += jnp.dot(kt[diag, :, half:], ds1, preferred_element_type=F32)
        in_steps(backward, jnp.int32(0))
        dq_ref[rows, :] = to_bf16((dqt[...] * scale).T)

    copies = [pltpu.make_async_copy(dq_ref, dq_hbm, io_sems.at[0])]
    copies[0].start()
    for b in range(blocks):
        for i in range(4):
            at = tile_rows(b, g ^ i)
            win[at, :] = to_bf16(acc[at, :])
            copy = pltpu.make_async_copy(
                win.at[at], out_refs[2 * b + i % 2].at[i // 2], sems.at[b, i]
            )
            copy.start()
            copies.append(copy)
    for copy in copies:
        copy.wait()


def along_ctx(x, by):
    n = lax.axis_size("ctx")
    return lax.ppermute(x, "ctx", [(i, i + by) for i in range(n) if 0 <= i + by < n])


def swap_grp(x, bit):
    n = lax.axis_size("grp")
    return lax.ppermute(x, "grp", [(i, i ^ bit) for i in range(n)])


def shards(queries, kv_cache, grad_out, doc_tiles):
    local_tiles = queries.shape[0] // TILE
    reach = (MAXT - 2) // local_tiles + 1
    assert reach == 3
    blocks = reach + 1
    slots = blocks * local_tiles
    scale = 1.0 / math.sqrt(DH)
    width = 2 * DH

    x0 = kv_cache
    y0 = swap_grp(x0, 2)
    x1 = along_ctx(x0, 1)
    x2 = along_ctx(x0, 2)
    x3 = along_ctx(x1, 2)
    y2 = along_ctx(y0, 2)
    y1 = swap_grp(x1, 2)
    y3 = swap_grp(x3, 2)
    pieces = []
    for x, y in ((x3, y3), (x2, y2), (x1, y1), (x0, y0)):
        pieces += [x, swap_grp(x, 1), y, swap_grp(y, 1)]

    hbm = pl.BlockSpec(memory_space=pl.ANY)
    half = jax.ShapeDtypeStruct((local_tiles // 2, TILE, width), BF16)
    grad_queries, *halves = pl.pallas_call(
        lambda *refs: local_kernel(*refs, local_tiles=local_tiles, reach=reach, scale=scale),
        out_shape=(jax.ShapeDtypeStruct(queries.shape, BF16),) + (half,) * (2 * blocks),
        in_specs=[pl.BlockSpec(memory_space=pltpu.SMEM)] + [hbm] * (2 + 4 * blocks),
        out_specs=(hbm,) * (1 + 2 * blocks),
        scratch_shapes=[
            pltpu.VMEM(queries.shape, BF16),
            pltpu.VMEM(queries.shape, BF16),
            pltpu.VMEM(queries.shape, BF16),
            pltpu.VMEM((slots * TILE, width), BF16),
            pltpu.VMEM((slots, DH, TILE), BF16),
            pltpu.VMEM((MAXT * TILE, TILE), F32),
            pltpu.VMEM((MAXT * TILE, TILE), F32),
            pltpu.VMEM((slots * TILE, width), F32),
            pltpu.VMEM((DH, TILE), F32),
            pltpu.SemaphoreType.DMA((blocks, 4)),
            pltpu.SemaphoreType.DMA((2,)),
        ],
        compiler_params=pltpu.CompilerParams(vmem_limit_bytes=56 * 1024 * 1024),
    )(doc_tiles, queries, grad_out, *pieces)

    mine, theirs = {}, {}
    for d in range(reach, -1, -1):
        keep, send = halves[2 * (reach - d)], halves[2 * (reach - d) + 1]
        got = swap_grp(send, 1)
        mine[d] = keep[0].astype(F32) + got[0].astype(F32)
        theirs[d] = keep[1].astype(F32) + got[1].astype(F32)
    far_theirs = along_ctx(to_bf16(theirs[2]), -2).astype(F32)
    far_mine = along_ctx(to_bf16(mine[2]), -2).astype(F32)
    third = mine[3] + swap_grp(to_bf16(theirs[3]), 2).astype(F32)
    third = along_ctx(to_bf16(third), -3).astype(F32)
    near = mine[1] + swap_grp(to_bf16(theirs[1]), 2).astype(F32)
    near = along_ctx(to_bf16(near), -1).astype(F32)
    own = mine[0] + swap_grp(to_bf16(theirs[0] + far_theirs), 2).astype(F32)
    own = own + far_mine + third + near
    grad_kv = to_bf16(jnp.concatenate([own[:, :DH] * scale, own[:, DH:]], axis=1))
    return (grad_queries, grad_kv)


def solution(mesh):
    placed = (P("ctx", "grp"), P(("ctx", "grp"), None), P("ctx", "grp"), P())
    return jax.shard_map(
        shards,
        mesh=mesh,
        in_specs=placed,
        out_specs=(P("ctx", "grp"), P(("ctx", "grp"), None)),
        check_vma=False,
    )
```

time: 137 us -> 107 us (0.78)
  starting transfers between devices: 76.7 us -> 43.2 us
  Pallas kernels: 21.2 us -> 25.3 us
    ppermute x6 -> x8, starting transfers between devices: 63.5 us -> 32.5 us  [along_ctx(): lax.ppermute(x, 'ctx', [(i, i + by) for i in range(n) if 0 <= i + by < n])]
    ppermute x20 -> x18, waiting for transfers between devices: 16.1 us -> 8.33 us  [swap_grp(): return lax.ppermute(x, 'grp', [(i, i ^ bit) for i in range(n)])]
    ppermute x6 -> x8, waiting for transfers between devices: 16.7 us -> 23.6 us  [along_ctx(): lax.ppermute(x, 'ctx', [(i, i + by) for i in range(n) if 0 <= i + by < n])]
    pallas_call x1, Pallas kernels: 21.2 us -> 25.3 us  [shards(): pl.pallas_call(lambda *refs: local_kernel(*refs, local_tiles=local_tiles,...]
    ppermute x20 -> x18, starting transfers between devices: 13.1 us -> 10.6 us  [swap_grp(): return lax.ppermute(x, 'grp', [(i, i ^ bit) for i in range(n)])]
  transfers between devices with their start and end apart: 26 -> 26, of which waited for: 11 -> 11; matrix products, arithmetic and copies ran while one was open for 1% -> 2% of each run, Pallas kernels for 0% -> 0%
where the time goes in v1:
time: 107 us; the launch traced here: 105 us
  starting transfers between devices  43.2 us (40%)
  waiting for transfers between devices  31.9 us (30%)
  Pallas kernels  25.3 us (24%)
  other arithmetic  2.63 us (2%)
    ppermute x8, starting transfers between devices, along_ctx(): lax.ppermute(x, 'ctx', [(i, i + by) for i in range(n) if 0 <= i + by < n])  32.5 us
    pallas_call x1, Pallas kernels, shards(): pl.pallas_call(lambda *refs: local_kernel(*refs, local_tiles=local_tiles,...  25.3 us
    ppermute x8, waiting for transfers between devices, along_ctx(): lax.ppermute(x, 'ctx', [(i, i + by) for i in range(n) if 0 <= i + by < n])  23.6 us
    ppermute x18, starting transfers between devices, swap_grp(): return lax.ppermute(x, 'grp', [(i, i ^ bit) for i in range(n)])  10.6 us
    ppermute x18, waiting for transfers between devices, swap_grp(): return lax.ppermute(x, 'grp', [(i, i ^ bit) for i in range(n)])  8.33 us
  transfers between devices with their start and end apart: 26, of which 11 were waited for; matrix products, arithmetic and copies ran while one was open for 2% of the time, Pallas kernels for 0%

profile of v1, /device:TPU:16, one launch (start us, length us, event | category | flops | bytes accessed | tf_op | source)
XLA Modules:
  0.0 104.8 jit_solution(10140335375538239005)
XLA Ops:
  0.6 3.4 %collective-permute-start = (bf16[512,256]{1,0:T(8,128)(2,1)}, bf16[512,256]{1,0:T(8,128)(2,1)S(1)}, u32[]{:S(2)}, u32[]{:S(2)}) collective-permute-start(bf16[512,256]{1,0:T(8,128)(2,1)} %refs_15_.1), channel_id=1, source_target_pairs={{0,4},{4,8},{8,12},{12,16},{16,20},{20,24},{24,28},{1,5},{5,9},{9,... | collective-permute-start | bytes 786440 | tf_op jit(solution)/shard_map/ppermute | solution.py:225
  4.0 1.6 %collective-permute-start.7 = (bf16[512,256]{1,0:T(8,128)(2,1)}, bf16[512,256]{1,0:T(8,128)(2,1)S(1)}, u32[]{:S(2)}, u32[]{:S(2)}) collective-permute-start(bf16[512,256]{1,0:T(8,128)(2,1)} %refs_15_.1), channel_id=1, source_target_pairs={{0,2},{1,3},{2,0},{3,1},{4,6},{5,7},{6,4},{7,5},{8,10},{9,11},{10,... | collective-permute-start | bytes 786440 | tf_op jit(solution)/shard_map/ppermute | solution.py:230
  5.6 3.5 %collective-permute-start.5 = (bf16[512,256]{1,0:T(8,128)(2,1)}, bf16[512,256]{1,0:T(8,128)(2,1)S(1)}, u32[]{:S(2)}, u32[]{:S(2)}) collective-permute-start(bf16[512,256]{1,0:T(8,128)(2,1)} %refs_15_.1), channel_id=1, source_target_pairs={{0,8},{4,12},{8,16},{12,20},{16,24},{20,28},{1,9},{5,13},{9,17},{1... | collective-permute-start | bytes 786440 | tf_op jit(solution)/shard_map/ppermute | solution.py:225
  9.1 0.1 collective-permute-start.13
  9.2 3.5 %collective-permute-done.refs_11_ = bf16[512,256]{1,0:T(8,128)(2,1)S(1)} collective-permute-done((bf16[512,256]{1,0:T(8,128)(2,1)}, bf16[512,256]{1,0:T(8,128)(2,1)S(1)}, u32[]{:S(2)}, u32[]{:S(2)}) %collective-permute-start) | collective-permute-done | bytes 262176 | tf_op jit(solution)/shard_map/ppermute | solution.py:225
  12.7 3.6 %collective-permute-start.1 = (bf16[512,256]{1,0:T(8,128)(2,1)S(1)}, bf16[512,256]{1,0:T(8,128)(2,1)S(1)}, u32[]{:S(2)}, u32[]{:S(2)}) collective-permute-start(bf16[512,256]{1,0:T(8,128)(2,1)S(1)} %collective-permute-done.refs_11_), channel_id=1, source_target_pairs={{0,8},{4,12},{8,16},{12,20},{16,24},{20,28},{1,9},{5,13},{9,17},{1... | collective-permute-start | bytes 786440 | tf_op jit(solution)/shard_map/ppermute | solution.py:225
  16.3 0.0 collective-permute-done.7.refs_17_
  16.3 0.1 collective-permute-start.14
  16.4 1.9 %collective-permute-start.8 = (bf16[512,256]{1,0:T(8,128)(2,1)S(1)}, bf16[512,256]{1,0:T(8,128)(2,1)S(1)}, u32[]{:S(2)}, u32[]{:S(2)}) collective-permute-start(bf16[512,256]{1,0:T(8,128)(2,1)S(1)} %collective-permute-done.7.refs_17_), channel_id=1, source_target_pairs={{0,8},{4,12},{8,16},{12,20},{16,24},{20,28},{1,9},{5,13},{9,17},{1... | collective-permute-start | bytes 786440 | tf_op jit(solution)/shard_map/ppermute | solution.py:225
  18.3 0.0 collective-permute-done.5.refs_7_
  18.4 0.6 collective-permute-start.6
  18.9 0.0 collective-permute-done.13.refs_16_
  18.9 1.5 %collective-permute-start.11 = (bf16[512,256]{1,0:T(8,128)(2,1)S(1)}, bf16[512,256]{1,0:T(8,128)(2,1)S(1)}, u32[]{:S(2)}, u32[]{:S(2)}) collective-permute-start(bf16[512,256]{1,0:T(8,128)(2,1)S(1)} %collective-permute-done.refs_11_), channel_id=1, source_target_pairs={{0,2},{1,3},{2,0},{3,1},{4,6},{5,7},{6,4},{7,5},{8,10},{9,11},{10,... | collective-permute-start | bytes 786440 | tf_op jit(solution)/shard_map/ppermute | solution.py:230
  20.4 0.7 collective-permute-done.1.refs_3_
  21.1 1.5 %collective-permute-start.3 = (bf16[512,256]{1,0:T(8,128)(2,1)S(1)}, bf16[512,256]{1,0:T(8,128)(2,1)S(1)}, u32[]{:S(2)}, u32[]{:S(2)}) collective-permute-start(bf16[512,256]{1,0:T(8,128)(2,1)S(1)} %collective-permute-done.1.refs_3_), channel_id=1, source_target_pairs={{0,2},{1,3},{2,0},{3,1},{4,6},{5,7},{6,4},{7,5},{8,10},{9,11},{10,... | collective-permute-start | bytes 786440 | tf_op jit(solution)/shard_map/ppermute | solution.py:230
  22.6 0.0 collective-permute-done.14.refs_18_
  22.6 0.0 collective-permute-start.10
  22.6 4.4 %collective-permute-done.8.refs_9_ = bf16[512,256]{1,0:T(8,128)(2,1)S(1)} collective-permute-done((bf16[512,256]{1,0:T(8,128)(2,1)S(1)}, bf16[512,256]{1,0:T(8,128)(2,1)S(1)}, u32[]{:S(2)}, u32[]{:S(2)}) %collective-permute-start.8) | collective-permute-done | bytes 262176 | tf_op jit(solution)/shard_map/ppermute | solution.py:225
  27.0 0.0 collective-permute-start.2
  27.0 0.0 collective-permute-done.6.refs_8_
  27.0 0.5 collective-permute-start.9
  27.5 0.6 collective-permute-done.11.refs_13_
  28.1 0.0 collective-permute-start.12
  28.1 4.8 %collective-permute-done.3.refs_5_ = bf16[512,256]{1,0:T(8,128)(2,1)S(1)} collective-permute-done((bf16[512,256]{1,0:T(8,128)(2,1)S(1)}, bf16[512,256]{1,0:T(8,128)(2,1)S(1)}, u32[]{:S(2)}, u32[]{:S(2)}) %collective-permute-start.3) | collective-permute-done | bytes 262176 | tf_op jit(solution)/shard_map/ppermute | solution.py:230
  32.8 0.0 collective-permute-start.4
  32.8 0.0 collective-permute-done.10.refs_12_
  32.9 0.0 collective-permute-done.9.refs_10_
  32.9 0.0 collective-permute-done.12.refs_14_
  32.9 0.0 collective-permute-done.2.refs_4_
  32.9 0.0 copy-start.14
  32.9 1.5 %collective-permute-done.4.refs_6_ = bf16[512,256]{1,0:T(8,128)(2,1)S(1)} collective-permute-done((bf16[512,256]{1,0:T(8,128)(2,1)S(1)}, bf16[512,256]{1,0:T(8,128)(2,1)S(1)}, u32[]{:S(2)}, u32[]{:S(2)}) %collective-permute-start.4) | collective-permute-done | bytes 262176 | tf_op jit(solution)/shard_map/ppermute | solution.py:230
  34.4 0.0 copy-done.6
  34.5 0.7 copy-done.17
  35.2 25.3 %shard_map.59 = (bf16[2048,128]{1,0:T(8,128)(2,1)}, bf16[2,512,256]{2,1,0:T(8,128)(2,1)}, bf16[2,512,256]{2,1,0:T(8,128)(2,1)}, bf16[2,512,256]{2,1,0:T(8,128)(2...) custom-call(s32[4]{0:T(128)} %refs_0_.1, ...), custom_call_target="tpu_custom_call" | custom-call | tf_op jit(solution)/shard_map/pallas_call | solution.py:256
  60.5 0.2 collective-permute-start.16
  60.7 0.4 collective-permute-start.20
  61.1 0.1 collective-permute-start.23
  61.2 0.4 collective-permute-start.15
  61.6 1.1 %collective-permute-done.16 = bf16[2,512,256]{2,1,0:T(8,128)(2,1)S(1)} collective-permute-done((bf16[2,512,256]{2,1,0:T(8,128)(2,1)}, bf16[2,512,256]{2,1,0:T(8,128)(2,1)S(1)}, u32[]{:S(2)}, u32[]{:S(2)}) %collective-permute-start.16) | collective-permute-done | bytes 524320 | tf_op jit(solution)/shard_map/ppermute | solution.py:230
  62.7 1.2 %fusion.6 = (bf16[512,256]{1,0:T(8,128)(2,1)S(1)}, bf16[512,256]{1,0:T(8,128)(2,1)S(1)}) fusion(bf16[2,512,256]{2,1,0:T(8,128)(2,1)S(1)} %collective-permute-done.16, bf16[2,512,256]{2,1,0:T(8,128)(2,1)} %get-tuple-element.14), kind=kLoop, calls=%fused_computation.14 | loop fusion | flops 1048576 | bytes 1572864 | tf_op jit(solution)/shard_map/convert_element_type | solution.py:20
  63.9 2.1 %collective-permute-start.17 = (bf16[512,256]{1,0:T(8,128)(2,1)S(1)}, bf16[512,256]{1,0:T(8,128)(2,1)S(1)}, u32[]{:S(2)}, u32[]{:S(2)}) collective-permute-start(bf16[512,256]{1,0:T(8,128)(2,1)S(1)} %get-tuple-element.20), channel_id=1, source_target_pairs={{8,0},{12,4},{16,8},{20,12},{24,16},{28,20},{9,1},{13,5},{17,9},{2... | collective-permute-start | bytes 786440 | tf_op jit(solution)/shard_map/ppermute | solution.py:225
  66.0 1.9 %collective-permute-start.19 = (bf16[512,256]{1,0:T(8,128)(2,1)S(1)}, bf16[512,256]{1,0:T(8,128)(2,1)S(1)}, u32[]{:S(2)}, u32[]{:S(2)}) collective-permute-start(bf16[512,256]{1,0:T(8,128)(2,1)S(1)} %get-tuple-element.21), channel_id=1, source_target_pairs={{8,0},{12,4},{16,8},{20,12},{24,16},{28,20},{9,1},{13,5},{17,9},{2... | collective-permute-start | bytes 786440 | tf_op jit(solution)/shard_map/ppermute | solution.py:225
  67.9 0.0 collective-permute-done.20
  67.9 0.1 fusion.8
  68.0 1.6 %collective-permute-start.21 = (bf16[512,256]{1,0:T(8,128)(2,1)S(1)}, bf16[512,256]{1,0:T(8,128)(2,1)S(1)}, u32[]{:S(2)}, u32[]{:S(2)}) collective-permute-start(bf16[512,256]{1,0:T(8,128)(2,1)S(1)} %fusion.8), channel_id=1, source_target_pairs={{0,2},{1,3},{2,0},{3,1},{4,6},{5,7},{6,4},{7,5},{8,10},{9,11},{10,... | collective-permute-start | bytes 786440 | tf_op jit(solution)/shard_map/ppermute | solution.py:230
  69.6 0.0 collective-permute-done.23
  69.6 0.1 fusion.9
  69.7 0.6 collective-permute-start.24
  70.2 0.0 collective-permute-done.15
  70.2 4.8 %collective-permute-done.17 = bf16[512,256]{1,0:T(8,128)(2,1)S(1)} collective-permute-done((bf16[512,256]{1,0:T(8,128)(2,1)S(1)}, bf16[512,256]{1,0:T(8,128)(2,1)S(1)}, u32[]{:S(2)}, u32[]{:S(2)}) %collective-permute-start.17) | collective-permute-done | bytes 262176 | tf_op jit(solution)/shard_map/ppermute | solution.py:225
  75.1 0.1 fusion.2
  75.2 1.6 %collective-permute-start.18 = (bf16[512,256]{1,0:T(8,128)(2,1)S(1)}, bf16[512,256]{1,0:T(8,128)(2,1)S(1)}, u32[]{:S(2)}, u32[]{:S(2)}) collective-permute-start(bf16[512,256]{1,0:T(8,128)(2,1)S(1)} %fusion.2), channel_id=1, source_target_pairs={{0,2},{1,3},{2,0},{3,1},{4,6},{5,7},{6,4},{7,5},{8,10},{9,11},{10,... | collective-permute-start | bytes 786440 | tf_op jit(solution)/shard_map/ppermute | solution.py:230
  76.8 0.4 collective-permute-done.21
  77.2 0.1 fusion.1
  77.3 5.7 %collective-permute-start.22 = (bf16[512,256]{1,0:T(8,128)(2,1)S(1)}, bf16[512,256]{1,0:T(8,128)(2,1)S(1)}, u32[]{:S(2)}, u32[]{:S(2)}) collective-permute-start(bf16[512,256]{1,0:T(8,128)(2,1)S(1)} %fusion.1), channel_id=1, source_target_pairs={{12,0},{16,4},{20,8},{24,12},{28,16},{13,1},{17,5},{21,9},{25,13},... | collective-permute-start | bytes 786440 | tf_op jit(solution)/shard_map/ppermute | solution.py:225
  83.1 0.0 collective-permute-done.24
  83.1 0.1 fusion
  83.2 10.4 %collective-permute-start.25 = (bf16[512,256]{1,0:T(8,128)(2,1)S(1)}, bf16[512,256]{1,0:T(8,128)(2,1)S(1)}, u32[]{:S(2)}, u32[]{:S(2)}) collective-permute-start(bf16[512,256]{1,0:T(8,128)(2,1)S(1)} %fusion), channel_id=1, source_target_pairs={{4,0},{8,4},{12,8},{16,12},{20,16},{24,20},{28,24},{5,1},{9,5},{13... | collective-permute-start | bytes 786440 | tf_op jit(solution)/shard_map/ppermute | solution.py:225
  93.6 0.0 collective-permute-done.19
  93.6 0.0 collective-permute-done.18
  93.6 4.6 %collective-permute-done.22 = bf16[512,256]{1,0:T(8,128)(2,1)S(1)} collective-permute-done((bf16[512,256]{1,0:T(8,128)(2,1)S(1)}, bf16[512,256]{1,0:T(8,128)(2,1)S(1)}, u32[]{:S(2)}, u32[]{:S(2)}) %collective-permute-start.22) | collective-permute-done | bytes 262176 | tf_op jit(solution)/shard_map/ppermute | solution.py:225
  98.3 5.5 %collective-permute-done.25 = bf16[512,256]{1,0:T(8,128)(2,1)S(1)} collective-permute-done((bf16[512,256]{1,0:T(8,128)(2,1)S(1)}, bf16[512,256]{1,0:T(8,128)(2,1)S(1)}, u32[]{:S(2)}, u32[]{:S(2)}) %collective-permute-start.25) | collective-permute-done | bytes 262176 | tf_op jit(solution)/shard_map/ppermute | solution.py:225
  103.8 0.2 fusion.5
  104.1 0.7 pad_maximum_fusion
  (35 shorter events, 0.1 us)
Async XLA Ops:
  0.6 12.1 %collective-permute-start = (bf16[512,256]{1,0:T(8,128)(2,1)}, bf16[512,256]{1,0:T(8,128)(2,1)S(1)}, u32[]{:S(2)}, u32[]{:S(2)}) collective-permute-start(bf16[512,256]{1,0:T(8,128)(2,1)} %refs_15_.1), channel_id=1, source_target_pairs={{0,4},{4,8},{8,12},{12,16},{16,20},{20,24},{24,28},{1,5},{5,9},{9,... | collective-permute-start | bytes 786440 | tf_op jit(solution)/shard_map/ppermute | solution.py:225
  4.0 12.3 %collective-permute-start.7 = (bf16[512,256]{1,0:T(8,128)(2,1)}, bf16[512,256]{1,0:T(8,128)(2,1)S(1)}, u32[]{:S(2)}, u32[]{:S(2)}) collective-permute-start(bf16[512,256]{1,0:T(8,128)(2,1)} %refs_15_.1), channel_id=1, source_target_pairs={{0,2},{1,3},{2,0},{3,1},{4,6},{5,7},{6,4},{7,5},{8,10},{9,11},{10,... | collective-permute-start | bytes 786440 | tf_op jit(solution)/shard_map/ppermute | solution.py:230
  5.6 12.7 %collective-permute-start.5 = (bf16[512,256]{1,0:T(8,128)(2,1)}, bf16[512,256]{1,0:T(8,128)(2,1)S(1)}, u32[]{:S(2)}, u32[]{:S(2)}) collective-permute-start(bf16[512,256]{1,0:T(8,128)(2,1)} %refs_15_.1), channel_id=1, source_target_pairs={{0,8},{4,12},{8,16},{12,20},{16,24},{20,28},{1,9},{5,13},{9,17},{1... | collective-permute-start | bytes 786440 | tf_op jit(solution)/shard_map/ppermute | solution.py:225
  9.1 9.8 %collective-permute-start.13 = (bf16[512,256]{1,0:T(8,128)(2,1)}, bf16[512,256]{1,0:T(8,128)(2,1)S(1)}, u32[]{:S(2)}, u32[]{:S(2)}) collective-permute-start(bf16[512,256]{1,0:T(8,128)(2,1)} %refs_15_.1), channel_id=1, source_target_pairs={{0,1},{1,0},{2,3},{3,2},{4,5},{5,4},{6,7},{7,6},{8,9},{9,8},{10,11... | collective-permute-start | bytes 786440 | tf_op jit(solution)/shard_map/ppermute | solution.py:230
  12.7 21.7 %copy-start.3 = (bf16[512,256]{1,0:T(8,128)(2,1)}, bf16[512,256]{1,0:T(8,128)(2,1)S(1)}, u32[]{:S(2)}) copy-start(bf16[512,256]{1,0:T(8,128)(2,1)S(1)} %collective-permute-done.refs_11_) | copy-start | bytes 786436
  12.7 8.4 %collective-permute-start.1 = (bf16[512,256]{1,0:T(8,128)(2,1)S(1)}, bf16[512,256]{1,0:T(8,128)(2,1)S(1)}, u32[]{:S(2)}, u32[]{:S(2)}) collective-permute-start(bf16[512,256]{1,0:T(8,128)(2,1)S(1)} %collective-permute-done.refs_11_), channel_id=1, source_target_pairs={{0,8},{4,12},{8,16},{12,20},{16,24},{20,28},{1,9},{5,13},{9,17},{1... | collective-permute-start | bytes 786440 | tf_op jit(solution)/shard_map/ppermute | solution.py:225
  16.3 18.1 %copy-start.4 = (bf16[512,256]{1,0:T(8,128)(2,1)}, bf16[512,256]{1,0:T(8,128)(2,1)S(1)}, u32[]{:S(2)}) copy-start(bf16[512,256]{1,0:T(8,128)(2,1)S(1)} %collective-permute-done.7.refs_17_) | copy-start | bytes 786436
  16.3 6.3 %collective-permute-start.14 = (bf16[512,256]{1,0:T(8,128)(2,1)S(1)}, bf16[512,256]{1,0:T(8,128)(2,1)S(1)}, u32[]{:S(2)}, u32[]{:S(2)}) collective-permute-start(bf16[512,256]{1,0:T(8,128)(2,1)S(1)} %collective-permute-done.7.refs_17_), channel_id=1, source_target_pairs={{0,1},{1,0},{2,3},{3,2},{4,5},{5,4},{6,7},{7,6},{8,9},{9,8},{10,11... | collective-permute-start | bytes 786440 | tf_op jit(solution)/shard_map/ppermute | solution.py:230
  16.4 10.6 %collective-permute-start.8 = (bf16[512,256]{1,0:T(8,128)(2,1)S(1)}, bf16[512,256]{1,0:T(8,128)(2,1)S(1)}, u32[]{:S(2)}, u32[]{:S(2)}) collective-permute-start(bf16[512,256]{1,0:T(8,128)(2,1)S(1)} %collective-permute-done.7.refs_17_), channel_id=1, source_target_pairs={{0,8},{4,12},{8,16},{12,20},{16,24},{20,28},{1,9},{5,13},{9,17},{1... | collective-permute-start | bytes 786440 | tf_op jit(solution)/shard_map/ppermute | solution.py:225
  18.3 16.0 %copy-start.5 = (bf16[512,256]{1,0:T(8,128)(2,1)}, bf16[512,256]{1,0:T(8,128)(2,1)S(1)}, u32[]{:S(2)}) copy-start(bf16[512,256]{1,0:T(8,128)(2,1)S(1)} %collective-permute-done.5.refs_7_) | copy-start | bytes 786436
  18.4 8.6 %collective-permute-start.6 = (bf16[512,256]{1,0:T(8,128)(2,1)S(1)}, bf16[512,256]{1,0:T(8,128)(2,1)S(1)}, u32[]{:S(2)}, u32[]{:S(2)}) collective-permute-start(bf16[512,256]{1,0:T(8,128)(2,1)S(1)} %collective-permute-done.5.refs_7_), channel_id=1, source_target_pairs={{0,1},{1,0},{2,3},{3,2},{4,5},{5,4},{6,7},{7,6},{8,9},{9,8},{10,11... | collective-permute-start | bytes 786440 | tf_op jit(solution)/shard_map/ppermute | solution.py:230
  18.9 15.5 %copy-start.6 = (bf16[512,256]{1,0:T(8,128)(2,1)}, bf16[512,256]{1,0:T(8,128)(2,1)S(1)}, u32[]{:S(2)}) copy-start(bf16[512,256]{1,0:T(8,128)(2,1)S(1)} %collective-permute-done.13.refs_16_) | copy-start | bytes 786436
  18.9 9.2 %collective-permute-start.11 = (bf16[512,256]{1,0:T(8,128)(2,1)S(1)}, bf16[512,256]{1,0:T(8,128)(2,1)S(1)}, u32[]{:S(2)}, u32[]{:S(2)}) collective-permute-start(bf16[512,256]{1,0:T(8,128)(2,1)S(1)} %collective-permute-done.refs_11_), channel_id=1, source_target_pairs={{0,2},{1,3},{2,0},{3,1},{4,6},{5,7},{6,4},{7,5},{8,10},{9,11},{10,... | collective-permute-start | bytes 786440 | tf_op jit(solution)/shard_map/ppermute | solution.py:230
  21.1 13.3 %copy-start.7 = (bf16[512,256]{1,0:T(8,128)(2,1)}, bf16[512,256]{1,0:T(8,128)(2,1)S(1)}, u32[]{:S(2)}) copy-start(bf16[512,256]{1,0:T(8,128)(2,1)S(1)} %collective-permute-done.1.refs_3_) | copy-start | bytes 786436
  21.1 11.7 %collective-permute-start.3 = (bf16[512,256]{1,0:T(8,128)(2,1)S(1)}, bf16[512,256]{1,0:T(8,128)(2,1)S(1)}, u32[]{:S(2)}, u32[]{:S(2)}) collective-permute-start(bf16[512,256]{1,0:T(8,128)(2,1)S(1)} %collective-permute-done.1.refs_3_), channel_id=1, source_target_pairs={{0,2},{1,3},{2,0},{3,1},{4,6},{5,7},{6,4},{7,5},{8,10},{9,11},{10,... | collective-permute-start | bytes 786440 | tf_op jit(solution)/shard_map/ppermute | solution.py:230
  22.6 11.8 %copy-start.8 = (bf16[512,256]{1,0:T(8,128)(2,1)}, bf16[512,256]{1,0:T(8,128)(2,1)S(1)}, u32[]{:S(2)}) copy-start(bf16[512,256]{1,0:T(8,128)(2,1)S(1)} %collective-permute-done.14.refs_18_) | copy-start | bytes 786436
  22.6 10.2 %collective-permute-start.10 = (bf16[512,256]{1,0:T(8,128)(2,1)S(1)}, bf16[512,256]{1,0:T(8,128)(2,1)S(1)}, u32[]{:S(2)}, u32[]{:S(2)}) collective-permute-start(bf16[512,256]{1,0:T(8,128)(2,1)S(1)} %collective-permute-done.refs_11_), channel_id=1, source_target_pairs={{0,1},{1,0},{2,3},{3,2},{4,5},{5,4},{6,7},{7,6},{8,9},{9,8},{10,11... | collective-permute-start | bytes 786440 | tf_op jit(solution)/shard_map/ppermute | solution.py:230
  27.0 7.4 %copy-start.9 = (bf16[512,256]{1,0:T(8,128)(2,1)}, bf16[512,256]{1,0:T(8,128)(2,1)S(1)}, u32[]{:S(2)}) copy-start(bf16[512,256]{1,0:T(8,128)(2,1)S(1)} %collective-permute-done.8.refs_9_) | copy-start | bytes 786436
  27.0 5.9 %collective-permute-start.2 = (bf16[512,256]{1,0:T(8,128)(2,1)S(1)}, bf16[512,256]{1,0:T(8,128)(2,1)S(1)}, u32[]{:S(2)}, u32[]{:S(2)}) collective-permute-start(bf16[512,256]{1,0:T(8,128)(2,1)S(1)} %collective-permute-done.1.refs_3_), channel_id=1, source_target_pairs={{0,1},{1,0},{2,3},{3,2},{4,5},{5,4},{6,7},{7,6},{8,9},{9,8},{10,11... | collective-permute-start | bytes 786440 | tf_op jit(solution)/shard_map/ppermute | solution.py:230
  27.0 7.4 %copy-start.10 = (bf16[512,256]{1,0:T(8,128)(2,1)}, bf16[512,256]{1,0:T(8,128)(2,1)S(1)}, u32[]{:S(2)}) copy-start(bf16[512,256]{1,0:T(8,128)(2,1)S(1)} %collective-permute-done.6.refs_8_) | copy-start | bytes 786436
  27.0 5.8 %collective-permute-start.9 = (bf16[512,256]{1,0:T(8,128)(2,1)S(1)}, bf16[512,256]{1,0:T(8,128)(2,1)S(1)}, u32[]{:S(2)}, u32[]{:S(2)}) collective-permute-start(bf16[512,256]{1,0:T(8,128)(2,1)S(1)} %collective-permute-done.8.refs_9_), channel_id=1, source_target_pairs={{0,1},{1,0},{2,3},{3,2},{4,5},{5,4},{6,7},{7,6},{8,9},{9,8},{10,11... | collective-permute-start | bytes 786440 | tf_op jit(solution)/shard_map/ppermute | solution.py:230
  28.1 6.4 %copy-start.11 = (bf16[512,256]{1,0:T(8,128)(2,1)}, bf16[512,256]{1,0:T(8,128)(2,1)S(1)}, u32[]{:S(2)}) copy-start(bf16[512,256]{1,0:T(8,128)(2,1)S(1)} %collective-permute-done.11.refs_13_) | copy-start | bytes 786436
  28.1 4.8 %collective-permute-start.12 = (bf16[512,256]{1,0:T(8,128)(2,1)S(1)}, bf16[512,256]{1,0:T(8,128)(2,1)S(1)}, u32[]{:S(2)}, u32[]{:S(2)}) collective-permute-start(bf16[512,256]{1,0:T(8,128)(2,1)S(1)} %collective-permute-done.11.refs_13_), channel_id=1, source_target_pairs={{0,1},{1,0},{2,3},{3,2},{4,5},{5,4},{6,7},{7,6},{8,9},{9,8},{10,11... | collective-permute-start | bytes 786440 | tf_op jit(solution)/shard_map/ppermute | solution.py:230
  32.8 1.6 %copy-start.12 = (bf16[512,256]{1,0:T(8,128)(2,1)}, bf16[512,256]{1,0:T(8,128)(2,1)S(1)}, u32[]{:S(2)}) copy-start(bf16[512,256]{1,0:T(8,128)(2,1)S(1)} %collective-permute-done.3.refs_5_) | copy-start | bytes 786436
  32.8 1.5 %collective-permute-start.4 = (bf16[512,256]{1,0:T(8,128)(2,1)S(1)}, bf16[512,256]{1,0:T(8,128)(2,1)S(1)}, u32[]{:S(2)}, u32[]{:S(2)}) collective-permute-start(bf16[512,256]{1,0:T(8,128)(2,1)S(1)} %collective-permute-done.3.refs_5_), channel_id=1, source_target_pairs={{0,1},{1,0},{2,3},{3,2},{4,5},{5,4},{6,7},{7,6},{8,9},{9,8},{10,11... | collective-permute-start | bytes 786440 | tf_op jit(solution)/shard_map/ppermute | solution.py:230
  32.8 1.6 %copy-start.13 = (bf16[512,256]{1,0:T(8,128)(2,1)}, bf16[512,256]{1,0:T(8,128)(2,1)S(1)}, u32[]{:S(2)}) copy-start(bf16[512,256]{1,0:T(8,128)(2,1)S(1)} %collective-permute-done.10.refs_12_) | copy-start | bytes 786436
  32.9 1.6 %copy-start.15 = (bf16[512,256]{1,0:T(8,128)(2,1)}, bf16[512,256]{1,0:T(8,128)(2,1)S(1)}, u32[]{:S(2)}) copy-start(bf16[512,256]{1,0:T(8,128)(2,1)S(1)} %collective-permute-done.9.refs_10_) | copy-start | bytes 786436
  32.9 1.6 %copy-start.16 = (bf16[512,256]{1,0:T(8,128)(2,1)}, bf16[512,256]{1,0:T(8,128)(2,1)S(1)}, u32[]{:S(2)}) copy-start(bf16[512,256]{1,0:T(8,128)(2,1)S(1)} %collective-permute-done.12.refs_14_) | copy-start | bytes 786436
  32.9 1.6 %copy-start.14 = (bf16[512,256]{1,0:T(8,128)(2,1)}, bf16[512,256]{1,0:T(8,128)(2,1)S(1)}, u32[]{:S(2)}) copy-start(bf16[512,256]{1,0:T(8,128)(2,1)S(1)} %collective-permute-done.2.refs_4_) | copy-start | bytes 786436
  34.5 0.7 copy-start.17
  60.5 2.2 %collective-permute-start.16 = (bf16[2,512,256]{2,1,0:T(8,128)(2,1)}, bf16[2,512,256]{2,1,0:T(8,128)(2,1)S(1)}, u32[]{:S(2)}, u32[]{:S(2)}) collective-permute-start(bf16[2,512,256]{2,1,0:T(8,128)(2,1)} %get-tuple-element.15), channel_id=1, source_target_pairs={{0,1},{1,0},{2,3},{3,2},{4,5},{5,4},{6,7},{7,6},{8,9},{9,8},{10,11... | collective-permute-start | bytes 1572872 | tf_op jit(solution)/shard_map/ppermute | solution.py:230
  60.7 7.2 %collective-permute-start.20 = (bf16[2,512,256]{2,1,0:T(8,128)(2,1)}, bf16[2,512,256]{2,1,0:T(8,128)(2,1)S(1)}, u32[]{:S(2)}, u32[]{:S(2)}) collective-permute-start(bf16[2,512,256]{2,1,0:T(8,128)(2,1)} %get-tuple-element.17), channel_id=1, source_target_pairs={{0,1},{1,0},{2,3},{3,2},{4,5},{5,4},{6,7},{7,6},{8,9},{9,8},{10,11... | collective-permute-start | bytes 1572872 | tf_op jit(solution)/shard_map/ppermute | solution.py:230
  61.1 8.5 %collective-permute-start.23 = (bf16[2,512,256]{2,1,0:T(8,128)(2,1)}, bf16[2,512,256]{2,1,0:T(8,128)(2,1)S(1)}, u32[]{:S(2)}, u32[]{:S(2)}) collective-permute-start(bf16[2,512,256]{2,1,0:T(8,128)(2,1)} %get-tuple-element.19), channel_id=1, source_target_pairs={{0,1},{1,0},{2,3},{3,2},{4,5},{5,4},{6,7},{7,6},{8,9},{9,8},{10,11... | collective-permute-start | bytes 1572872 | tf_op jit(solution)/shard_map/ppermute | solution.py:230
  61.2 9.1 %collective-permute-start.15 = (bf16[2,512,256]{2,1,0:T(8,128)(2,1)}, bf16[2,512,256]{2,1,0:T(8,128)(2,1)S(1)}, u32[]{:S(2)}, u32[]{:S(2)}) collective-permute-start(bf16[2,512,256]{2,1,0:T(8,128)(2,1)} %get-tuple-element.13), channel_id=1, source_target_pairs={{0,1},{1,0},{2,3},{3,2},{4,5},{5,4},{6,7},{7,6},{8,9},{9,8},{10,11... | collective-permute-start | bytes 1572872 | tf_op jit(solution)/shard_map/ppermute | solution.py:230
  62.7 5.2 %copy-start.1 = (bf16[2,512,256]{2,1,0:T(8,128)(2,1)S(1)}, bf16[2,512,256]{2,1,0:T(8,128)(2,1)}, u32[]{:S(2)}) copy-start(bf16[2,512,256]{2,1,0:T(8,128)(2,1)} %get-tuple-element.16) | copy-start | bytes 1572868
  63.9 5.7 %copy-start = (bf16[2,512,256]{2,1,0:T(8,128)(2,1)S(1)}, bf16[2,512,256]{2,1,0:T(8,128)(2,1)}, u32[]{:S(2)}) copy-start(bf16[2,512,256]{2,1,0:T(8,128)(2,1)} %get-tuple-element.18) | copy-start | bytes 1572868
  63.9 11.2 %collective-permute-start.17 = (bf16[512,256]{1,0:T(8,128)(2,1)S(1)}, bf16[512,256]{1,0:T(8,128)(2,1)S(1)}, u32[]{:S(2)}, u32[]{:S(2)}) collective-permute-start(bf16[512,256]{1,0:T(8,128)(2,1)S(1)} %get-tuple-element.20), channel_id=1, source_target_pairs={{8,0},{12,4},{16,8},{20,12},{24,16},{28,20},{9,1},{13,5},{17,9},{2... | collective-permute-start | bytes 786440 | tf_op jit(solution)/shard_map/ppermute | solution.py:225
  66.0 27.7 %collective-permute-start.19 = (bf16[512,256]{1,0:T(8,128)(2,1)S(1)}, bf16[512,256]{1,0:T(8,128)(2,1)S(1)}, u32[]{:S(2)}, u32[]{:S(2)}) collective-permute-start(bf16[512,256]{1,0:T(8,128)(2,1)S(1)} %get-tuple-element.21), channel_id=1, source_target_pairs={{8,0},{12,4},{16,8},{20,12},{24,16},{28,20},{9,1},{13,5},{17,9},{2... | collective-permute-start | bytes 786440 | tf_op jit(solution)/shard_map/ppermute | solution.py:225
  68.0 7.1 %copy-start.2 = (bf16[2,512,256]{2,1,0:T(8,128)(2,1)S(1)}, bf16[2,512,256]{2,1,0:T(8,128)(2,1)}, u32[]{:S(2)}) copy-start(bf16[2,512,256]{2,1,0:T(8,128)(2,1)} %get-tuple-element.12) | copy-start | bytes 1572868
  68.0 9.2 %collective-permute-start.21 = (bf16[512,256]{1,0:T(8,128)(2,1)S(1)}, bf16[512,256]{1,0:T(8,128)(2,1)S(1)}, u32[]{:S(2)}, u32[]{:S(2)}) collective-permute-start(bf16[512,256]{1,0:T(8,128)(2,1)S(1)} %fusion.8), channel_id=1, source_target_pairs={{0,2},{1,3},{2,0},{3,1},{4,6},{5,7},{6,4},{7,5},{8,10},{9,11},{10,... | collective-permute-start | bytes 786440 | tf_op jit(solution)/shard_map/ppermute | solution.py:230
  69.7 13.4 %collective-permute-start.24 = (bf16[512,256]{1,0:T(8,128)(2,1)S(1)}, bf16[512,256]{1,0:T(8,128)(2,1)S(1)}, u32[]{:S(2)}, u32[]{:S(2)}) collective-permute-start(bf16[512,256]{1,0:T(8,128)(2,1)S(1)} %fusion.9), channel_id=1, source_target_pairs={{0,2},{1,3},{2,0},{3,1},{4,6},{5,7},{6,4},{7,5},{8,10},{9,11},{10,... | collective-permute-start | bytes 786440 | tf_op jit(solution)/shard_map/ppermute | solution.py:230
  75.2 18.4 %collective-permute-start.18 = (bf16[512,256]{1,0:T(8,128)(2,1)S(1)}, bf16[512,256]{1,0:T(8,128)(2,1)S(1)}, u32[]{:S(2)}, u32[]{:S(2)}) collective-permute-start(bf16[512,256]{1,0:T(8,128)(2,1)S(1)} %fusion.2), channel_id=1, source_target_pairs={{0,2},{1,3},{2,0},{3,1},{4,6},{5,7},{6,4},{7,5},{8,10},{9,11},{10,... | collective-permute-start | bytes 786440 | tf_op jit(solution)/shard_map/ppermute | solution.py:230
  77.3 21.0 %collective-permute-start.22 = (bf16[512,256]{1,0:T(8,128)(2,1)S(1)}, bf16[512,256]{1,0:T(8,128)(2,1)S(1)}, u32[]{:S(2)}, u32[]{:S(2)}) collective-permute-start(bf16[512,256]{1,0:T(8,128)(2,1)S(1)} %fusion.1), channel_id=1, source_target_pairs={{12,0},{16,4},{20,8},{24,12},{28,16},{13,1},{17,5},{21,9},{25,13},... | collective-permute-start | bytes 786440 | tf_op jit(solution)/shard_map/ppermute | solution.py:225
  83.2 20.6 %collective-permute-start.25 = (bf16[512,256]{1,0:T(8,128)(2,1)S(1)}, bf16[512,256]{1,0:T(8,128)(2,1)S(1)}, u32[]{:S(2)}, u32[]{:S(2)}) collective-permute-start(bf16[512,256]{1,0:T(8,128)(2,1)S(1)} %fusion), channel_id=1, source_target_pairs={{4,0},{8,4},{12,8},{16,12},{20,16},{24,20},{28,24},{5,1},{9,5},{13... | collective-permute-start | bytes 786440 | tf_op jit(solution)/shard_map/ppermute | solution.py:225
